TPU v7x, 256 devices: a whole 4x4x8 slice. The times are simulated.
256 devices in a mesh: dp: 32 (over x, z), mp: 8 (over y, core).
Axes of the slice: x: 4, y: 4, z: 8, core: 2. Of those that a mesh axis runs over, the one named last changes fastest.
Arguments:
- hidden_acts: bfloat16 [16384, 16384], P('dp', 'mp'), may hold values from -40 to 40
- out_grads: bfloat16 [16384, 2048], P(('dp', 'mp')), may hold values from -40 to 40
- left_stats: float32 [8, 64, 512, 512], P('mp', 'dp'), may hold values from -1 to 40, as said below
- right_stats: float32 [8, 64, 512, 512], P('mp', 'dp'), may hold values from -1 to 40, as said below
- block_owner: int32 [16], replicated, may hold values from 0 to 31, as said below
- block_slot: int32 [16], replicated, may hold values from 0 to 1, as said below
Outputs:
- update: bfloat16 [8, 16, 512, 512], P('mp', None, 'dp')
Inputs may be any that keep to these rules, and one draw needn't show every extreme that they name: `block_owner`: with block_slot, no two blocks share an (owner, slot) pair; an owner with a block in slot s has blocks in every lower slot; some owner holds 2 blocks. `block_slot`: the block's place among its owner's blocks. `left_stats`: each [512, 512] matrix is symmetric, with a positive diagonal entry larger than the sum of magnitudes of the rest of its row. `right_stats`: each [512, 512] matrix is symmetric, with a positive diagonal entry larger than the sum of magnitudes of the rest of its row.
All inputs are finite; a program needn't handle non-finite values. Where the computation divides by a largest or mean magnitude, that divisor is 1e-20 or more.
Results may differ from a plain program's by a relative error of at most 0.0044.
The roundings to bfloat16 on the way count: a program that leaves them out, or rounds other values in their place, can miss the bound.
Values may be sent and summed in bfloat16 or wider, within the bound.
A program may use at most 128 MiB of HBM per device.

v0:
```python
import math

import jax
import jax.numpy as jnp
from jax import lax
from jax.experimental import pallas as pl
from jax.experimental.pallas import tpu as pltpu
from jax.sharding import PartitionSpec as P

B = 512
CAP = 2
NX = 4
NZ = 8
NY = 4
DP = NX * NZ
MP = 2 * NY
GR = 4
GC = 4
NBLK = GR * GC
TOK = 512
SUB = TOK // MP
WIDTH = B // DP
XROWS = B // NX
F32 = jnp.float32
BF16 = jnp.bfloat16
MESH = pl.DeviceIdType.MESH

A_TIMES = (0.0, 0.02, 0.04, 0.06)
OWN_TIMES = (0.01, 0.03, 0.05, 0.07)
H_TIMES = (7.5, 11.0, 13.05, 14.9)
FIND_TIME = 1.0
HID_TIME = 14.95
STAT_TIME = 50.0
RELAY_TIMES = (6.5, 6.65, 7.2, 7.4)
NEAR_TIMES = (6.6, 6.7, 13.1, 19.1)
FAR_TIMES = (9.5, 10.5, 15.3, 19.15)
MIDDLE_TIMES = (
    (8.0, 12.0, 12.1, 13.0), (10.6, 14.0, 14.1, 15.2),
    (20.2, 21.0, 21.1, 23.0), (23.1, 26.5, 26.6, 28.5),
)
LAST_TIMES = (15.0, 19.0, 25.0, 30.5)
PREPARE_TIMES = (18.0, 23.5)
TILES = (
    (18.1, 0, 0), (20.5, 0, 1), (23.6, 1, 0), (23.7, 1, 1),
    (27.0, 0, 2), (27.2, 1, 2), (33.0, 0, 3), (33.2, 1, 3),
)
HOP_TIME = 1.35
HOP_DELAY = 1.7


def ring_order():
    waiting = [(t + 0.8, p, c, -1) for t, p, c in TILES]
    order, free = [], 0.0
    while waiting:
        waiting.sort()
        t, p, c, k = waiting.pop(0)
        if k >= 0:
            order.append((t, p, c, k))
        if k < 3:
            free = max(t, free) + HOP_TIME * (0.25, 0.5, 1.0, 1.0)[k + 1]
            waiting.append((free + HOP_DELAY, p, c, k + 1))
    return order


def dot(a, b, ca=1, cb=0):
    return lax.dot_general(a, b, (((ca,), (cb,)), ((), ())), preferred_element_type=F32)


def root_less_identity(matrix, eye):
    column_sums = jnp.sum(jnp.abs(matrix), axis=0, keepdims=True)
    scaling = 1.0 / (jnp.max(column_sums) + 1e-06)
    e1 = 0.25 * eye - (0.25 * scaling) * matrix
    e1b = e1.astype(BF16)
    e2 = dot(e1b, e1b)
    e2b = e2.astype(BF16)
    e34 = dot(e2b, (4.75 * e1 + e2).astype(BF16))
    return e1 + 2.5 * e2 + dot(e2b, (7.5 * e1 + 8.75 * e2 + e34).astype(BF16))


def body_kernel(
    hid, og, left, right, owner, slot, out,
    cg, hx, ht, tile, cw, ccw, early, landed, g16, send, mine, upd, arr, lbuf, rbuf, chosen,
    loc, a_s, a_r, h_s, h_r, b1_s, b1_r, b2_s, b2_r, s_s, s_r, r_s, r_r, g_s, g_r, u_s, u_r,
):
    i = lax.axis_index("dp")
    m = lax.axis_index("mp")
    x = i // NZ
    z = i % NZ
    core = m % 2
    sib = m + 1 - 2 * core
    up = (m + 2) % MP
    down = (m + MP - 2) % MP
    far = (m + 4) % MP
    factor = 1.0 / math.sqrt(B * TOK * DP)

    def remote(src, dst, ss, rs, dp, mp):
        return pltpu.make_async_remote_copy(
            src_ref=src, dst_ref=dst, send_sem=ss, recv_sem=rs,
            device_id=(dp, mp), device_id_type=MESH,
        )

    def wait(ref, sem):
        pltpu.make_async_copy(ref, ref, sem).wait()

    def peer(d):
        return ((x + d // NZ) % NX) * NZ + (z + d % NZ) % NZ

    def xpeer(d):
        return ((x + d) % NX) * NZ + z

    znext = x * NZ + (z + 1) % NZ
    zprev = x * NZ + (z + NZ - 1) % NZ

    def cols(r, xx):
        return pl.ds(pl.multiple_of(r * B + xx * XROWS, XROWS), XROWS)

    stat_copies = [
        pltpu.make_async_copy(left.at[0], lbuf, loc.at[0]),
        pltpu.make_async_copy(right.at[0], rbuf, loc.at[1]),
    ]
    own_copies = [
        pltpu.make_async_copy(og.at[:, pl.ds(c * B, B)], cg.at[c, x, m], loc.at[2 + c])
        for c in range(GC)
    ]
    hid_copies = [
        pltpu.make_async_copy(
            hid.at[:, cols(r, x)], hx.at[x, :, pl.ds(r * XROWS, XROWS)], loc.at[6 + r]
        )
        for r in range(GR)
    ]
    for copy in own_copies:
        copy.start()

    barrier = pltpu.get_barrier_semaphore()
    greeted = [(xpeer(d), m) for d in (1, 2, 3)]
    greeted += [(znext, m), (zprev, m), (i, up), (i, down), (i, sib)]
    for target in greeted:
        pl.semaphore_signal(barrier, inc=1, device_id=target, device_id_type=MESH)
    pl.semaphore_wait(barrier, len(greeted))

    def slab(q):
        return (x + q) % NX

    def a_copy(c, d):
        ss, rs = a_s.at[c, 3 - d], a_r.at[c, 3 - d]
        if d == 2:
            step = 1 + 2 * (c % 2)
            ref = cg.at[c, slab(4 - step), m]
            return remote(ref, ref, ss, rs, xpeer(step), m)
        return remote(og.at[:, pl.ds(c * B, B)], cg.at[c, x, m], ss, rs, xpeer(d), m)

    def h_copy(r, d):
        return remote(
            hid.at[:, cols(r, (x + d) % NX)], hx.at[x, :, pl.ds(r * XROWS, XROWS)],
            h_s.at[r, d - 1], h_r.at[r, d - 1], xpeer(d), m,
        )

    def b1(c, k, q):
        src = og.at[:, pl.ds(c * B, B)] if q == 0 else cg.at[c, slab(q), m]
        return remote(
            src, cg.at[c, slab(q), m], b1_s.at[c, k, q], b1_r.at[c, k, q], i, (up, down)[k]
        )

    def b2(c, q):
        k = q // 2
        ref = cg.at[c, slab(q), (down, up)[k]]
        return remote(ref, ref, b2_s.at[c, q], b2_r.at[c, q], i, (up, down)[k])

    def share(c, n):
        ref = cg.at[c, :, (m, down, up, far)[n]]
        return remote(ref, ref, s_s.at[c, n], s_r.at[c, n], i, sib)

    def send_a(c):
        for d in (1, 3):
            a_copy(c, d).start()

    def send_h(r):
        for d in (1, 3, 2):
            h_copy(r, d).start()

    def send_own(c):
        b1(c, 0, 0).start()
        b1(c, 1, 0).start()

    def relay(c):
        step = 1 + 2 * (c % 2)
        a_copy(c, step).wait_recv()
        a_copy(c, 2).start()

    def near(c):
        step = 1 + 2 * (c % 2)
        for d in (step, 4 - step):
            if d != step:
                a_copy(c, d).wait_recv()
            b1(c, 0, 4 - d).start()
            b1(c, 1, 4 - d).start()

    def far_one(c):
        a_copy(c, 2).wait_recv()
        b1(c, 0, 2).start()
        b1(c, 1, 2).start()
        own_copies[c].wait()
        share(c, 0).start()

    def middle(c, q):
        for k in (0, 1):
            b1(c, k, q).wait_recv()
            if k == q // 2:
                b2(c, q).start()
        if q == 2:
            share(c, 1).start()
            share(c, 2).start()

    def last(c):
        for q in range(NX):
            b2(c, q).wait_recv()
        share(c, 3).start()

    def prepare_hidden(p):
        for r in (2 * p, 2 * p + 1):
            hid_copies[r].wait()
            for d in (1, 3, 2):
                h_copy(r, d).wait_recv()
        half = pl.ds(2 * p * XROWS, 2 * XROWS)
        for n in range(NX):
            ht[half, pl.ds(n * TOK, TOK)] = hx[n, :, half].T

    def hop(ring, p, c, k):
        buf = (cw, ccw)[ring]
        target = (znext, zprev)[ring]
        ss, rs = r_s.at[ring, p, c, k], r_r.at[ring, p, c, k]
        if k < 2:
            rows = pl.ds(2 * p, 2) if k else 2 * p + ring
            return remote(
                early.at[ring, c, k, rows], landed.at[ring, c, k, rows], ss, rs, target, m
            )
        pair = pl.ds(2 * p, 2)
        return remote(buf.at[c, k - 2, pair], buf.at[c, k - 1, pair], ss, rs, target, m)

    seen = set()

    def multiply(p, c):
        if c not in seen:
            for n in range(4):
                share(c, n).wait_recv()
            seen.add(c)
        total = dot(ht[pl.ds(2 * p * XROWS, 2 * XROWS)], cg[c].reshape(NX * TOK, B))
        for r in range(2):
            for zz in range(NZ):
                start = r * XROWS + zz * WIDTH
                tile[c, zz, 2 * p + r] = total[start : start + WIDTH]
        for ring in (0, 1):
            row = 2 * p + ring
            early[ring, c, 0, row] = tile[c, (z + 4) % NZ, row].astype(BF16)
            hop(ring, p, c, 0).start()

    def ring_step(p, c, k):
        for ring in (0, 1):
            buf = (cw, ccw)[ring]
            hop(ring, p, c, k).wait_recv()
            chunk = (z + 3 - k) % NZ if ring == 0 else (z + NZ - 3 + k) % NZ
            pair = pl.ds(2 * p, 2)
            if k == 0:
                same, other = 2 * p + ring, 2 * p + 1 - ring
                summed = landed[ring, c, 0, same].astype(F32) + tile[c, chunk, same]
                early[ring, c, 1, same] = summed.astype(BF16)
                early[ring, c, 1, other] = tile[c, chunk, other].astype(BF16)
            elif k == 1:
                buf[c, 0, pair] = landed[ring, c, 1, pair].astype(F32) + tile[c, chunk, pair]
            else:
                buf[c, 1, pair] = buf[c, 1, pair] + tile[c, chunk, pair]
            hop(ring, p, c, k + 1).start()

    def ring_end(p, c):
        for ring in (0, 1):
            hop(ring, p, c, 3).wait_recv()
        pair = pl.ds(2 * p, 2)
        total = (tile[c, z, pair] + cw[c, 2, pair]) + ccw[c, 2, pair]
        total = (total * factor).astype(BF16)
        for r in range(2):
            g16[(2 * p + r) * GC + c] = total[r]

    def find_chosen():
        positions = [owner[j] * CAP + slot[j] for j in range(NBLK)]

        def find(p, carry):
            found = jnp.int32(0)
            for j in range(NBLK):
                found = jnp.where(positions[j] == p, j, found)
            chosen[p] = found
            return carry

        lax.fori_loop(0, DP * CAP, find, 0)

    def start_local(copies):
        for copy in copies:
            copy.start()

    plan = [(t, send_a, (c,)) for c, t in enumerate(A_TIMES)]
    plan += [(t, send_own, (c,)) for c, t in enumerate(OWN_TIMES)]
    plan += [(t, send_h, (r,)) for r, t in enumerate(H_TIMES)]
    plan += [(FIND_TIME, find_chosen, ()), (HID_TIME, start_local, (hid_copies,)), (STAT_TIME, start_local, (stat_copies,))]
    for c in range(GC):
        plan.append((RELAY_TIMES[c], relay, (c,)))
        plan.append((NEAR_TIMES[c], near, (c,)))
        plan.append((FAR_TIMES[c], far_one, (c,)))
        for q, t in zip((0, 3, 1, 2), MIDDLE_TIMES[c]):
            plan.append((t, middle, (c, q)))
        plan.append((LAST_TIMES[c], last, (c,)))
    plan += [(t, prepare_hidden, (p,)) for p, t in enumerate(PREPARE_TIMES)]
    for t, p, c in TILES:
        plan.append((t, multiply, (p, c)))
    for t, p, c, k in ring_order():
        plan.append((t, ring_step, (p, c, k)) if k < 3 else (t, ring_end, (p, c)))
    for _, action, args in sorted(plan, key=lambda entry: entry[0]):
        action(*args)

    rows_me = pl.ds(pl.multiple_of(i * WIDTH, WIDTH), WIDTH)
    for s in range(CAP):

        def deliver(d, carry):
            e = peer(d)
            send[s, e] = g16[chosen[e * CAP + s]]
            remote(
                send.at[s, e], mine.at[s, rows_me], g_s.at[s], g_r.at[s], e, m
            ).start()
            return carry

        lax.fori_loop(1, DP, deliver, 0)
        if s == 0:
            wait(mine.at[s, pl.ds(0, (DP - 1) * WIDTH)], g_s.at[s])
        mine[s, rows_me] = g16[chosen[i * CAP + s]]
    for copy in stat_copies:
        copy.wait()

    all_but_one = pl.ds(0, (DP - 1) * WIDTH)

    def refresh(s, carry):
        wait(mine.at[s, all_but_one], g_r.at[s])
        row = lax.broadcasted_iota(jnp.int32, (B, B), 0)
        col = lax.broadcasted_iota(jnp.int32, (B, B), 1)
        eye = jnp.where(row == col, 1.0, 0.0).astype(F32)
        grad = mine[s]
        wl = root_less_identity(lbuf[s] + dot(grad, grad, 1, 1), eye).astype(BF16)
        wr = root_less_identity(rbuf[s] + dot(grad, grad, 0, 0), eye).astype(BF16)
        half = grad.astype(F32) + dot(wl, grad)
        full = half + dot(half.astype(BF16), wr)
        scale = lax.rsqrt(jnp.sum(full * full) * (1.0 / (B * B)) + 1e-06)
        upd[s] = (full * scale).astype(BF16)

        def give(d, inner):
            e = peer(d)
            rows = pl.ds(pl.multiple_of(e * WIDTH, WIDTH), WIDTH)
            remote(upd.at[s, rows], arr.at[s, i], u_s.at[s], u_r.at[s], e, m).start()
            return inner

        lax.fori_loop(1, DP, give, 0)
        arr[s, i] = upd[s, rows_me]
        return carry

    lax.fori_loop(0, CAP, refresh, 0)

    for s in range(CAP):
        wait(arr.at[s, pl.ds(0, DP - 1)], u_r.at[s])
    for j in range(NBLK):
        out[j] = arr[slot[j], owner[j]]

    for s in range(CAP):
        if s > 0:
            wait(mine.at[s, all_but_one], g_s.at[s])
        wait(mine.at[s, all_but_one], u_s.at[s])
    for c in range(GC):
        for d in range(1, NX):
            a_copy(c, d).wait_send()
            h_copy(c, d).wait_send()
        for q in range(NX):
            b1(c, 0, q).wait_send()
            b1(c, 1, q).wait_send()
            b2(c, q).wait_send()
            share(c, q).wait_send()
        for ring in range(2):
            for p in range(2):
                for k in range(4):
                    hop(ring, p, c, k).wait_send()


def body(hidden_acts, out_grads, left_stats, right_stats, block_owner, block_slot):
    hbm = pl.BlockSpec(memory_space=pl.ANY)
    smem = pl.BlockSpec(memory_space=pltpu.SMEM)
    vmem = pl.BlockSpec(memory_space=pltpu.VMEM)
    dma = pltpu.SemaphoreType.DMA
    result = pl.pallas_call(
        body_kernel,
        out_shape=jax.ShapeDtypeStruct((NBLK, WIDTH, B), BF16),
        in_specs=[hbm, hbm, hbm, hbm, smem, smem],
        out_specs=vmem,
        scratch_shapes=[
            pltpu.VMEM((GC, NX, MP, SUB, B), BF16),
            pltpu.VMEM((NX, TOK, GR * XROWS), BF16),
            pltpu.VMEM((GR * XROWS, NX * TOK), BF16),
            pltpu.VMEM((GC, NZ, GR, WIDTH, B), F32),
            pltpu.VMEM((GC, 3, GR, WIDTH, B), F32),
            pltpu.VMEM((GC, 3, GR, WIDTH, B), F32),
            pltpu.VMEM((2, GC, 2, GR, WIDTH, B), BF16),
            pltpu.VMEM((2, GC, 2, GR, WIDTH, B), BF16),
            pltpu.VMEM((NBLK, WIDTH, B), BF16),
            pltpu.VMEM((CAP, DP, WIDTH, B), BF16),
            pltpu.VMEM((CAP, B, B), BF16),
            pltpu.VMEM((CAP, B, B), BF16),
            pltpu.VMEM((CAP, DP, WIDTH, B), BF16),
            pltpu.VMEM((CAP, B, B), F32),
            pltpu.VMEM((CAP, B, B), F32),
            pltpu.SMEM((DP * CAP,), jnp.int32),
            dma((10,)),
            dma((GC, 3)), dma((GC, 3)),
            dma((GR, 3)), dma((GR, 3)),
            dma((GC, 2, NX)), dma((GC, 2, NX)),
            dma((GC, NX)), dma((GC, NX)),
            dma((GC, 4)), dma((GC, 4)),
            dma((2, 2, GC, 4)), dma((2, 2, GC, 4)),
            dma((CAP,)), dma((CAP,)),
            dma((CAP,)), dma((CAP,)),
        ],
        compiler_params=pltpu.CompilerParams(
            collective_id=0, has_side_effects=True, vmem_limit_bytes=60 * 1024 * 1024
        ),
        cost_estimate=pl.CostEstimate(
            flops=10 * 10**9, bytes_accessed=7 * 10**6, transcendentals=0
        ),
    )(hidden_acts, out_grads, left_stats, right_stats, block_owner, block_slot)
    return result[None]


def solution(mesh):
    in_specs = (
        P("dp", "mp"),
        P(("dp", "mp"), None),
        P("mp", "dp", None, None),
        P("mp", "dp", None, None),
        P(),
        P(),
    )
    out_specs = P("mp", None, "dp", None)
    return jax.shard_map(body, mesh=mesh, in_specs=in_specs, out_specs=out_specs, check_vma=False)
```

profile of v0, /device:TPU:8, one launch (start us, length us, event | category | flops | bytes accessed | tf_op | source)
XLA Modules:
  0.0 126.1 jit_solution(14353576393352317130)
XLA Ops:
  0.0 124.4 %shard_map.64 = bf16[16,16,512]{2,1,0:T(8,128)(2,1)} custom-call(bf16[512,2048]{1,0:T(8,128)(2,1)} %hid.1, bf16[64,2048]{1,0:T(8,128)(2,1)} %og.1, f32[1,2,512,512]{3,2,1,0:T(8,128)} %left.1, f32[1,2,512,512]{3,2,1,0:T(8,128)} %right.1, s32[16]{0:T(128)} %owner.1, s32[16]{0:T(128)} %slot.1), custom_call_target="tpu_custom_call" | custom-call | flops 10000000000 | bytes 7000000 | tf_op jit(solution)/shard_map/pallas_call | solution.py:392
  124.4 1.7 %copy.8 = bf16[1,16,16,512]{3,2,1,0:T(8,128)(2,1)} copy(bf16[1,16,16,512]{3,2,1,0:T(8,128)(2,1)} %bitcast.1) | data formatting | bytes 524288
where the time goes:
time: 127 us; the launch traced here: 126 us
  Pallas kernels  124 us (98%)
  local copies, waits for them, and re-layouts  1.67 us (1%)
    pallas_call x1, Pallas kernels, body(): pl.pallas_call(body_kernel, out_shape=jax.ShapeDtypeStruct((NBLK, WIDTH,...  124 us

commit v1 on v0

--- a/solution.py
+++ b/solution.py
@@ -30,40 +30,48 @@
 H_TIMES = (7.5, 11.0, 13.05, 14.9)
 FIND_TIME = 1.0
 HID_TIME = 14.95
-STAT_TIME = 50.0
+STAT_TIME = 55.0
 RELAY_TIMES = (6.5, 6.65, 7.2, 7.4)
-NEAR_TIMES = (6.6, 6.7, 13.1, 19.1)
-FAR_TIMES = (9.5, 10.5, 15.3, 19.15)
+NEAR_TIMES = (6.6, 6.7, 12.2, 25.3)
+FAR_TIMES = (9.5, 10.5, 13.05, 25.35)
 MIDDLE_TIMES = (
     (8.0, 12.0, 12.1, 13.0), (10.6, 14.0, 14.1, 15.2),
-    (20.2, 21.0, 21.1, 23.0), (23.1, 26.5, 26.6, 28.5),
+    (27.0, 27.1, 27.2, 29.0), (29.1, 33.5, 33.6, 35.5),
 )
-LAST_TIMES = (15.0, 19.0, 25.0, 30.5)
-PREPARE_TIMES = (18.0, 23.5)
+LAST_TIMES = (19.0, 25.2, 33.0, 38.5)
+PREPARE_TIMES = (23.0, 32.0)
 TILES = (
-    (18.1, 0, 0), (20.5, 0, 1), (23.6, 1, 0), (23.7, 1, 1),
-    (27.0, 0, 2), (27.2, 1, 2), (33.0, 0, 3), (33.2, 1, 3),
+    (24.0, 0, 0), (26.5, 0, 1), (32.1, 1, 0), (32.2, 1, 1),
+    (35.0, 0, 2), (35.1, 1, 2), (41.0, 0, 3), (41.2, 1, 3),
 )
-HOP_TIME = 1.35
-HOP_DELAY = 1.7
+HOP_TIMES = (0.37, 0.72, 1.4, 1.4)
+HOP_DELAY = 2.4
+LEAD = 1.0
 
 
 def ring_order():
     waiting = [(t + 0.8, p, c, -1) for t, p, c in TILES]
-    order, free = [], 0.0
+    order, free, now = [], 0.0, 0.0
     while waiting:
-        waiting.sort()
-        t, p, c, k = waiting.pop(0)
+        now = max(now, free - LEAD, min(waiting)[0])
+        entry = min((e for e in waiting if e[0] <= now), key=lambda e: (e[3], e[0]))
+        waiting.remove(entry)
+        _, p, c, k = entry
         if k >= 0:
-            order.append((t, p, c, k))
+            order.append((now, p, c, k))
         if k < 3:
-            free = max(t, free) + HOP_TIME * (0.25, 0.5, 1.0, 1.0)[k + 1]
+            free = max(now, free) + HOP_TIMES[k + 1]
             waiting.append((free + HOP_DELAY, p, c, k + 1))
     return order
 
 
 def dot(a, b, ca=1, cb=0):
     return lax.dot_general(a, b, (((ca,), (cb,)), ((), ())), preferred_element_type=F32)
+
+
+def split(value):
+    top = value.astype(BF16)
+    return top, (value - top.astype(F32)).astype(BF16)
 
 
 def root_less_identity(matrix, eye):
@@ -341,10 +349,11 @@
         col = lax.broadcasted_iota(jnp.int32, (B, B), 1)
         eye = jnp.where(row == col, 1.0, 0.0).astype(F32)
         grad = mine[s]
-        wl = root_less_identity(lbuf[s] + dot(grad, grad, 1, 1), eye).astype(BF16)
-        wr = root_less_identity(rbuf[s] + dot(grad, grad, 0, 0), eye).astype(BF16)
-        half = grad.astype(F32) + dot(wl, grad)
-        full = half + dot(half.astype(BF16), wr)
+        wl, wl_rest = split(root_less_identity(lbuf[s] + dot(grad, grad, 1, 1), eye))
+        wr, wr_rest = split(root_less_identity(rbuf[s] + dot(grad, grad, 0, 0), eye))
+        half = grad.astype(F32) + (dot(wl, grad) + dot(wl_rest, grad))
+        top, rest = split(half)
+        full = half + (dot(top, wr) + (dot(rest, wr) + dot(top, wr_rest)))
         scale = lax.rsqrt(jnp.sum(full * full) * (1.0 / (B * B)) + 1e-06)
         upd[s] = (full * scale).astype(BF16)
 

time: 127 us -> 126 us (level)
  no operation moved by 1% of the time
where the time goes in v1:
time: 126 us
  Pallas kernels  124 us (98%)
  local copies, waits for them, and re-layouts  1.67 us (1%)
    pallas_call x1, Pallas kernels, body(): pl.pallas_call(body_kernel, out_shape=jax.ShapeDtypeStruct((NBLK, WIDTH,...  124 us

profile of v1, /device:TPU:8, one launch (start us, length us, event | category | flops | bytes accessed | tf_op | source)
XLA Modules:
  0.0 126.0 jit_solution(10103509702738945723)
XLA Ops:
  0.0 124.3 %shard_map.64 = bf16[16,16,512]{2,1,0:T(8,128)(2,1)} custom-call(bf16[512,2048]{1,0:T(8,128)(2,1)} %hid.1, bf16[64,2048]{1,0:T(8,128)(2,1)} %og.1, f32[1,2,512,512]{3,2,1,0:T(8,128)} %left.1, f32[1,2,512,512]{3,2,1,0:T(8,128)} %right.1, s32[16]{0:T(128)} %owner.1, s32[16]{0:T(128)} %slot.1), custom_call_target="tpu_custom_call" | custom-call | flops 10000000000 | bytes 7000000 | tf_op jit(solution)/shard_map/pallas_call | solution.py:401
  124.3 1.7 %copy.8 = bf16[1,16,16,512]{3,2,1,0:T(8,128)(2,1)} copy(bf16[1,16,16,512]{3,2,1,0:T(8,128)(2,1)} %bitcast.1) | data formatting | bytes 524288

commit v2 on v1

--- a/solution.py
+++ b/solution.py
@@ -44,7 +44,7 @@
     (24.0, 0, 0), (26.5, 0, 1), (32.1, 1, 0), (32.2, 1, 1),
     (35.0, 0, 2), (35.1, 1, 2), (41.0, 0, 3), (41.2, 1, 3),
 )
-HOP_TIMES = (0.37, 0.72, 1.4, 1.4)
+HOP_TIMES = (0.37, 0.72, 0.72, 1.4)
 HOP_DELAY = 2.4
 LEAD = 1.0
 
@@ -237,13 +237,13 @@
         buf = (cw, ccw)[ring]
         target = (znext, zprev)[ring]
         ss, rs = r_s.at[ring, p, c, k], r_r.at[ring, p, c, k]
-        if k < 2:
+        if k < 3:
             rows = pl.ds(2 * p, 2) if k else 2 * p + ring
             return remote(
                 early.at[ring, c, k, rows], landed.at[ring, c, k, rows], ss, rs, target, m
             )
         pair = pl.ds(2 * p, 2)
-        return remote(buf.at[c, k - 2, pair], buf.at[c, k - 1, pair], ss, rs, target, m)
+        return remote(buf.at[c, 0, pair], buf.at[c, 1, pair], ss, rs, target, m)
 
     seen = set()
 
@@ -274,16 +274,17 @@
                 early[ring, c, 1, same] = summed.astype(BF16)
                 early[ring, c, 1, other] = tile[c, chunk, other].astype(BF16)
             elif k == 1:
-                buf[c, 0, pair] = landed[ring, c, 1, pair].astype(F32) + tile[c, chunk, pair]
+                summed = landed[ring, c, 1, pair].astype(F32) + tile[c, chunk, pair]
+                early[ring, c, 2, pair] = summed.astype(BF16)
             else:
-                buf[c, 1, pair] = buf[c, 1, pair] + tile[c, chunk, pair]
+                buf[c, 0, pair] = landed[ring, c, 2, pair].astype(F32) + tile[c, chunk, pair]
             hop(ring, p, c, k + 1).start()
 
     def ring_end(p, c):
         for ring in (0, 1):
             hop(ring, p, c, 3).wait_recv()
         pair = pl.ds(2 * p, 2)
-        total = (tile[c, z, pair] + cw[c, 2, pair]) + ccw[c, 2, pair]
+        total = (tile[c, z, pair] + cw[c, 1, pair]) + ccw[c, 1, pair]
         total = (total * factor).astype(BF16)
         for r in range(2):
             g16[(2 * p + r) * GC + c] = total[r]
@@ -343,6 +344,20 @@
 
     all_but_one = pl.ds(0, (DP - 1) * WIDTH)
 
+    for c in range(GC):
+        for d in range(1, NX):
+            a_copy(c, d).wait_send()
+            h_copy(c, d).wait_send()
+        for q in range(NX):
+            b1(c, 0, q).wait_send()
+            b1(c, 1, q).wait_send()
+            b2(c, q).wait_send()
+            share(c, q).wait_send()
+        for ring in range(2):
+            for p in range(2):
+                for k in range(4):
+                    hop(ring, p, c, k).wait_send()
+
     def refresh(s, carry):
         wait(mine.at[s, all_but_one], g_r.at[s])
         row = lax.broadcasted_iota(jnp.int32, (B, B), 0)
@@ -378,19 +393,6 @@
         if s > 0:
             wait(mine.at[s, all_but_one], g_s.at[s])
         wait(mine.at[s, all_but_one], u_s.at[s])
-    for c in range(GC):
-        for d in range(1, NX):
-            a_copy(c, d).wait_send()
-            h_copy(c, d).wait_send()
-        for q in range(NX):
-            b1(c, 0, q).wait_send()
-            b1(c, 1, q).wait_send()
-            b2(c, q).wait_send()
-            share(c, q).wait_send()
-        for ring in range(2):
-            for p in range(2):
-                for k in range(4):
-                    hop(ring, p, c, k).wait_send()
 
 
 def body(hidden_acts, out_grads, left_stats, right_stats, block_owner, block_slot):
@@ -408,10 +410,10 @@
             pltpu.VMEM((NX, TOK, GR * XROWS), BF16),
             pltpu.VMEM((GR * XROWS, NX * TOK), BF16),
             pltpu.VMEM((GC, NZ, GR, WIDTH, B), F32),
-            pltpu.VMEM((GC, 3, GR, WIDTH, B), F32),
-            pltpu.VMEM((GC, 3, GR, WIDTH, B), F32),
-            pltpu.VMEM((2, GC, 2, GR, WIDTH, B), BF16),
-            pltpu.VMEM((2, GC, 2, GR, WIDTH, B), BF16),
+            pltpu.VMEM((GC, 2, GR, WIDTH, B), F32),
+            pltpu.VMEM((GC, 2, GR, WIDTH, B), F32),
+            pltpu.VMEM((2, GC, 3, GR, WIDTH, B), BF16),
+            pltpu.VMEM((2, GC, 3, GR, WIDTH, B), BF16),
             pltpu.VMEM((NBLK, WIDTH, B), BF16),
             pltpu.VMEM((CAP, DP, WIDTH, B), BF16),
             pltpu.VMEM((CAP, B, B), BF16),

time: 126 us -> 124 us (0.984)
  Pallas kernels: 124 us -> 122 us
    pallas_call x1, Pallas kernels: 124 us -> 122 us  [body(): pl.pallas_call(body_kernel, out_shape=jax.ShapeDtypeStruct((NBLK, WIDTH,...]
where the time goes in v2:
time: 124 us; the launch traced here: 123 us
  Pallas kernels  122 us (98%)
  local copies, waits for them, and re-layouts  1.67 us (1%)
    pallas_call x1, Pallas kernels, body(): pl.pallas_call(body_kernel, out_shape=jax.ShapeDtypeStruct((NBLK, WIDTH,...  122 us

profile of v2, /device:TPU:8, one launch (start us, length us, event | category | flops | bytes accessed | tf_op | source)
XLA Modules:
  0.0 123.2 jit_solution(7214203775004892276)
XLA Ops:
  0.0 121.6 %shard_map.64 = bf16[16,16,512]{2,1,0:T(8,128)(2,1)} custom-call(bf16[512,2048]{1,0:T(8,128)(2,1)} %hid.1, bf16[64,2048]{1,0:T(8,128)(2,1)} %og.1, f32[1,2,512,512]{3,2,1,0:T(8,128)} %left.1, f32[1,2,512,512]{3,2,1,0:T(8,128)} %right.1, s32[16]{0:T(128)} %owner.1, s32[16]{0:T(128)} %slot.1), custom_call_target="tpu_custom_call" | custom-call | flops 10000000000 | bytes 7000000 | tf_op jit(solution)/shard_map/pallas_call | solution.py:403
  121.6 1.7 %copy.8 = bf16[1,16,16,512]{3,2,1,0:T(8,128)(2,1)} copy(bf16[1,16,16,512]{3,2,1,0:T(8,128)(2,1)} %bitcast.1) | data formatting | bytes 524288

commit v3 on v2

--- a/solution.py
+++ b/solution.py
@@ -336,8 +336,6 @@
             return carry
 
         lax.fori_loop(1, DP, deliver, 0)
-        if s == 0:
-            wait(mine.at[s, pl.ds(0, (DP - 1) * WIDTH)], g_s.at[s])
         mine[s, rows_me] = g16[chosen[i * CAP + s]]
     for copy in stat_copies:
         copy.wait()
@@ -390,8 +388,7 @@
         out[j] = arr[slot[j], owner[j]]
 
     for s in range(CAP):
-        if s > 0:
-            wait(mine.at[s, all_but_one], g_s.at[s])
+        wait(mine.at[s, all_but_one], g_s.at[s])
         wait(mine.at[s, all_but_one], u_s.at[s])
 
 

time: 124 us -> 124 us (level)
  no operation moved by 1% of the time
where the time goes in v3:
time: 124 us; the launch traced here: 122 us
  Pallas kernels  121 us (98%)
  local copies, waits for them, and re-layouts  1.67 us (1%)
    pallas_call x1, Pallas kernels, body(): pl.pallas_call(body_kernel, out_shape=jax.ShapeDtypeStruct((NBLK, WIDTH,...  121 us

profile of v3, /device:TPU:8, one launch (start us, length us, event | category | flops | bytes accessed | tf_op | source)
XLA Modules:
  0.0 122.2 jit_solution(488150666087723482)
XLA Ops:
  0.0 120.5 %shard_map.64 = bf16[16,16,512]{2,1,0:T(8,128)(2,1)} custom-call(bf16[512,2048]{1,0:T(8,128)(2,1)} %hid.1, bf16[64,2048]{1,0:T(8,128)(2,1)} %og.1, f32[1,2,512,512]{3,2,1,0:T(8,128)} %left.1, f32[1,2,512,512]{3,2,1,0:T(8,128)} %right.1, s32[16]{0:T(128)} %owner.1, s32[16]{0:T(128)} %slot.1), custom_call_target="tpu_custom_call" | custom-call | flops 10000000000 | bytes 7000000 | tf_op jit(solution)/shard_map/pallas_call | solution.py:400
  120.5 1.7 %copy.8 = bf16[1,16,16,512]{3,2,1,0:T(8,128)(2,1)} copy(bf16[1,16,16,512]{3,2,1,0:T(8,128)(2,1)} %bitcast.1) | data formatting | bytes 524288
